TPU v7x, 32 devices: a whole 2x2x4 slice. The times are simulated.
32 devices in a mesh: ens: 2 (over y), lon: 4 (over z), lat: 2 (over x), ch: 2 (over core).
Axes of the slice: x: 2, y: 2, z: 4, core: 2. Of those that a mesh axis runs over, the one named last changes fastest.
Arguments:
- inputs: bfloat16 [128, 4096, 768], P(('ens', 'lat'), 'lon', 'ch'), parts along dimension 0, may hold values from -6 to 6
- cotangent: bfloat16 [128, 4096, 768], P(('ens', 'lat'), 'lon', 'ch'), parts along dimension 0, may hold values from -12 to 12
- first_weight: bfloat16 [2, 4, 2, 96, 96], P('ch', 'lat'), may hold values from -0.4375 to 0.4375
- first_bias: float32 [2, 4, 2, 96], P('ch', 'lat'), may hold values from -3 to 3
- second_weight: bfloat16 [2, 4, 2, 96, 96], P('ch', 'lat'), may hold values from -0.4375 to 0.4375
- counts: int32 [2, 4], P('ch', 'lat'), may hold values from 16 to 32, as said below
- keep_flags: int32 [64, 32, 2, 4], P(None, 'lon', 'ch', 'lat'), may hold values 0 or 1
Outputs:
- input_grad: bfloat16 [128, 4096, 768], P(('ens', 'lat'), 'lon', 'ch'), parts along dimension 0
- first_grad: float32 [4, 4, 2, 96, 96], P(('ens', 'ch'), 'lat'), parts along dimension 0
- second_grad: float32 [4, 4, 2, 96, 96], P(('ens', 'ch'), 'lat'), parts along dimension 0
- first_bias_grad: float32 [4, 4, 2, 96], P(('ens', 'ch'), 'lat'), parts along dimension 0
- second_bias_grad: float32 [4, 4, 2, 96], P(('ens', 'ch'), 'lat'), parts along dimension 0
There are 2 independent parts, one for each index of `ens`. A program takes and returns all parts, laid end to end along the dimension named above; an argument that names none is the same for every part. Nothing has to cross between parts.
Inputs may be any that keep to these rules, and one draw needn't show every extreme that they name: Block b keeps longitude modes below counts[b]; some block keeps all 32 and some keeps 32 / 2.
All inputs are finite; a program needn't handle non-finite values. No bound on the sum of `keep_flags` on one device may be relied on, other than what follows from the above.
Results may differ from a plain program's by a relative error of at most 0.001.
Values may be sent and summed in bfloat16 or wider, within the bound.
A program may use at most 192 MiB of HBM per device.

v0:
```python
import functools
import math

import jax
import jax.numpy as jnp
from jax import lax
from jax.experimental import pallas as pl
from jax.experimental.pallas import tpu as pltpu
from jax.sharding import PartitionSpec as P
import ml_dtypes
import numpy as np

KM = 32


exact_precision = lax.Precision.HIGHEST


def wave_tables(modes, cells, length):
    phase = (modes[:, None] * cells[None, :] % length).astype(jnp.float32)
    angle = phase * (2.0 * math.pi / length)
    scale = 1.0 / math.sqrt(length)
    return (jnp.cos(angle) * scale, jnp.sin(angle) * scale)


def activate(real_part, imag_part):
    return (jax.nn.gelu(real_part, approximate=True), jax.nn.gelu(imag_part, approximate=True))


def mixing_grads(spec_real, spec_imag, error_real, error_imag, weight_mask, first, bias, second):
    first_real = first[:, 0].astype(jnp.float32)
    first_imag = first[:, 1].astype(jnp.float32)
    second_real = second[:, 0].astype(jnp.float32)
    second_imag = second[:, 1].astype(jnp.float32)

    def forward_mul(values, matrix):
        return jnp.einsum("rbi,bio->rbo", values, matrix, precision=exact_precision)

    def back_mul(values, matrix):
        return jnp.einsum("rbo,bio->rbi", values, matrix, precision=exact_precision)

    def outer_sum(left, right):
        return jnp.einsum("rbi,rbo->bio", left, right, precision=exact_precision)

    pre_real = (
        forward_mul(spec_real, first_real) - forward_mul(spec_imag, first_imag) + bias[None, :, 0]
    )
    pre_imag = (
        forward_mul(spec_real, first_imag) + forward_mul(spec_imag, first_real) + bias[None, :, 1]
    )
    (act_real, act_imag), backward = jax.vjp(activate, pre_real, pre_imag)
    out_real = error_real * weight_mask[..., None]
    out_imag = error_imag * weight_mask[..., None]
    hid_real = back_mul(out_real, second_real) + back_mul(out_imag, second_imag)
    hid_imag = back_mul(out_imag, second_real) - back_mul(out_real, second_imag)
    grad_real, grad_imag = backward((hid_real, hid_imag))
    in_real = back_mul(grad_real, first_real) + back_mul(grad_imag, first_imag)
    in_imag = back_mul(grad_imag, first_real) - back_mul(grad_real, first_imag)
    second_grad = jnp.stack(
        [
            outer_sum(act_real, out_real) + outer_sum(act_imag, out_imag),
            outer_sum(act_real, out_imag) - outer_sum(act_imag, out_real),
        ],
        axis=1,
    )
    first_grad = jnp.stack(
        [
            outer_sum(spec_real, grad_real) + outer_sum(spec_imag, grad_imag),
            outer_sum(spec_real, grad_imag) - outer_sum(spec_imag, grad_real),
        ],
        axis=1,
    )
    first_bias_grad = jnp.stack([jnp.sum(grad_real, axis=0), jnp.sum(grad_imag, axis=0)], axis=1)
    second_bias_grad = jnp.stack([jnp.sum(out_real, axis=0), jnp.sum(out_imag, axis=0)], axis=1)
    return (in_real, in_imag, first_grad, second_grad, first_bias_grad, second_bias_grad)


def lat_forward(lat_cos, lat_sin, real_part, imag_part):
    out_real = jnp.einsum(
        "qh,khc->kqc", lat_cos, real_part, precision=exact_precision
    ) + jnp.einsum("qh,khc->kqc", lat_sin, imag_part, precision=exact_precision)
    out_imag = jnp.einsum(
        "qh,khc->kqc", lat_cos, imag_part, precision=exact_precision
    ) - jnp.einsum("qh,khc->kqc", lat_sin, real_part, precision=exact_precision)
    return (out_real, out_imag)


def lat_adjoint(lat_cos, lat_sin, real_part, imag_part):
    out_real = jnp.einsum(
        "qh,kqc->khc", lat_cos, real_part, precision=exact_precision
    ) - jnp.einsum("qh,kqc->khc", lat_sin, imag_part, precision=exact_precision)
    out_imag = jnp.einsum(
        "qh,kqc->khc", lat_sin, real_part, precision=exact_precision
    ) + jnp.einsum("qh,kqc->khc", lat_cos, imag_part, precision=exact_precision)
    return (out_real, out_imag)


def on_device(inputs, cotangent, first_weight, first_bias, second_weight, counts, keep_flags):
    lat_rows, lon_cells, chan_local = inputs.shape
    lon_count = lax.axis_size("lon")
    lat_count = lax.axis_size("lat")
    lon_place = lax.axis_index("lon")
    modes_dev = KM // lon_count
    lon_total = lon_cells * lon_count
    lat_total = lat_rows * lat_count
    own_cells = lon_place * lon_cells + jnp.arange(lon_cells, dtype=jnp.int32)
    own_modes = lon_place * modes_dev + jnp.arange(modes_dev, dtype=jnp.int32)
    field_x = inputs.astype(jnp.float32)
    field_g = cotangent.astype(jnp.float32)
    cosine, sine = wave_tables(
        jnp.arange(modes_dev * lax.axis_size("lon"), dtype=jnp.int32), own_cells, lon_total
    )
    x_real = jnp.einsum("hwc,kw->khc", field_x, cosine, precision=exact_precision)
    x_imag = -jnp.einsum("hwc,kw->khc", field_x, sine, precision=exact_precision)
    g_real = jnp.einsum("hwc,kw->khc", field_g, cosine, precision=exact_precision)
    g_imag = -jnp.einsum("hwc,kw->khc", field_g, sine, precision=exact_precision)
    spectra = lax.psum_scatter(
        jnp.stack([x_real, x_imag, g_real, g_imag], axis=1), "lon", scatter_dimension=0, tiled=True
    )
    factor = jnp.where(own_modes == 0, 1.0, 2.0).astype(jnp.float32)
    unity = jnp.ones_like(factor)
    spectra = spectra * jnp.stack([unity, unity, factor, factor], axis=1)[:, :, None, None]
    blocks = lax.all_to_all(spectra, "lat", split_axis=3, concat_axis=2, tiled=True)
    chan_block = blocks.shape[3]
    block_size = first_weight.shape[-1]
    local_blocks = chan_block // block_size
    lat_index = jnp.arange(lat_total, dtype=jnp.int32)
    lat_cos, lat_sin = wave_tables(lat_index, lat_index, lat_total)
    spec_real, spec_imag = lat_forward(lat_cos, lat_sin, blocks[:, 0], blocks[:, 1])
    error_real, error_imag = lat_forward(lat_cos, lat_sin, blocks[:, 2], blocks[:, 3])
    rows = modes_dev * lat_total
    cut = (own_modes[:, None] < counts[0][None, :]).astype(jnp.float32)
    flags = jnp.transpose(keep_flags[:, :, 0, :].astype(jnp.float32), (1, 0, 2))
    weight_mask = (cut[:, None, :] * flags).reshape(rows, local_blocks)

    def as_rows(values):
        return values.reshape(rows, local_blocks, block_size)

    results = mixing_grads(
        as_rows(spec_real),
        as_rows(spec_imag),
        as_rows(error_real),
        as_rows(error_imag),
        weight_mask,
        first_weight[0],
        first_bias[0],
        second_weight[0],
    )
    in_real, in_imag, first_grad, second_grad, first_bias_grad, second_bias_grad = results
    first_grad, second_grad, first_bias_grad, second_bias_grad = lax.psum(
        (first_grad, second_grad, first_bias_grad, second_bias_grad), "lon"
    )
    back_real, back_imag = lat_adjoint(
        lat_cos,
        lat_sin,
        in_real.reshape(modes_dev, lat_total, chan_block),
        in_imag.reshape(modes_dev, lat_total, chan_block),
    )
    back = lax.all_to_all(
        jnp.stack([back_real, back_imag], axis=1), "lat", split_axis=2, concat_axis=3, tiled=True
    )
    piece = lax.all_gather(back, "lon", axis=0, tiled=True)
    cosine, sine = wave_tables(jnp.arange(piece.shape[0], dtype=jnp.int32), own_cells, lon_total)
    total = jnp.einsum("khc,kw->hwc", piece[:, 0], cosine, precision=exact_precision)
    input_grad = (
        total - jnp.einsum("khc,kw->hwc", piece[:, 1], sine, precision=exact_precision)
    ).astype(jnp.bfloat16)
    return (
        input_grad,
        first_grad[None],
        second_grad[None],
        first_bias_grad[None],
        second_bias_grad[None],
    )


MESH = pl.DeviceIdType.MESH
TOP = 32767.0
LEAST = 1e-30


def np_split(table):
    high = table.astype(ml_dtypes.bfloat16)
    low = (table - high.astype(np.float64)).astype(ml_dtypes.bfloat16)
    return high, low


def split(values):
    high = values.astype(jnp.bfloat16)
    low = (values - high.astype(jnp.float32)).astype(jnp.bfloat16)
    return high, low


def np_waves(modes, cells, length):
    angle = (modes[:, None] * cells[None, :] % length) * (2.0 * np.pi / length)
    return np.cos(angle) / np.sqrt(length), np.sin(angle) / np.sqrt(length)


def lon_table(length):
    cosine, sine = np_waves(np.arange(KM), np.arange(length), length)
    return np.stack([cosine, -sine], axis=1).reshape(2 * KM, length)


def lat_tables(length, modes):
    index = np.arange(length)
    cosine, sine = np_waves(index, index, length)
    there = np.zeros((2, 2, modes, length, length, 2, modes, 2))
    back = np.zeros((length, modes, 2, 2, modes, length))
    for k in range(modes):
        for f in range(2):
            there[f, 0, k, :, :, f, k, 0] = cosine
            there[f, 0, k, :, :, f, k, 1] = sine
            there[f, 1, k, :, :, f, k, 1] = cosine
            there[f, 1, k, :, :, f, k, 0] = -sine
        back[:, k, 0, 0, k, :] = cosine.T
        back[:, k, 0, 1, k, :] = -sine.T
        back[:, k, 1, 0, k, :] = sine.T
        back[:, k, 1, 1, k, :] = cosine.T
    rows = 4 * modes * length
    return there.reshape(rows, rows), back.reshape(rows // 2, rows // 2)


def dot(left, right, dims=((1,), (0,))):
    return lax.dot_general(left, right, (dims, ((), ())), preferred_element_type=jnp.float32)


def dot_exact_right(left, right, dims=((1,), (0,))):
    high, low = split(left)
    return dot(high, right, dims) + dot(low, right, dims)


def dot_both(left, right, dims=((1,), (0,))):
    left_high, left_low = left
    right_high, right_low = right
    return (
        dot(left_high, right_high, dims)
        + dot(left_high, right_low, dims)
        + dot(left_low, right_high, dims)
    )


def code(values):
    most = jnp.maximum(jnp.max(jnp.abs(values), axis=1, keepdims=True), LEAST)
    return jnp.round(values * (TOP / most)).astype(jnp.int32), most * (1.0 / TOP)


def pick(scales, lane):
    lanes = lax.broadcasted_iota(jnp.int32, scales.shape, scales.ndim - 1)
    return jnp.sum(jnp.where(lanes == lane, scales, 0.0), axis=-1, keepdims=True)


def place(lat_count):
    return lax.axis_index("lon") * lat_count + lax.axis_index("lat")


def device(number, lat_count):
    return {"lon": lax.div(number, lat_count), "lat": lax.rem(number, lat_count)}


def greet(group, lat_count):
    me = place(lat_count)
    barrier = pltpu.get_barrier_semaphore()
    for step in range(1, group):
        pl.semaphore_signal(
            barrier,
            inc=1,
            device_id=device(lax.rem(me + step, group), lat_count),
            device_id_type=MESH,
        )
    pl.semaphore_wait(barrier, group - 1)


def forward_kernel(
    group, lat_count, chunks, table_ref, factor_ref, x_ref, g_ref, sums_ref, scales_ref,
    send, scales, send_sem, recv_sem, own_sem, scale_send_sem, scale_recv_sem, scale_own_sem,
):
    step_now = pl.program_id(0)
    me = place(lat_count)
    per_chunk = x_ref.shape[0]
    rows = table_ref.shape[0] // 2
    own = rows // group

    def sums_copy(chunk, step, arriving):
        target = lax.rem(me + step, group)
        slot = lax.rem(me + group - step, group) if arriving else me
        here = pl.ds(chunk * per_chunk, per_chunk)
        return pltpu.make_async_remote_copy(
            src_ref=send.at[target, here],
            dst_ref=sums_ref.at[slot, here],
            send_sem=send_sem.at[chunk, step],
            recv_sem=recv_sem.at[chunk, step],
            device_id=device(target, lat_count),
            device_id_type=MESH,
        )

    def own_copy(chunk):
        here = pl.ds(chunk * per_chunk, per_chunk)
        return pltpu.make_async_copy(send.at[me, here], sums_ref.at[me, here], own_sem.at[chunk])

    def scales_copy(step, arriving):
        target = lax.rem(me + step, group)
        slot = lax.rem(me + group - step, group) if arriving else me
        return pltpu.make_async_remote_copy(
            src_ref=scales.at[target],
            dst_ref=scales_ref.at[slot],
            send_sem=scale_send_sem.at[step],
            recv_sem=scale_recv_sem.at[step],
            device_id=device(target, lat_count),
            device_id_type=MESH,
        )

    @pl.when(step_now == 0)
    def _():
        greet(group, lat_count)
        scales[...] = jnp.zeros_like(scales)

    table = table_ref[...]
    lanes = lax.broadcasted_iota(jnp.int32, (own, 128), 1)
    for inside in range(per_chunk):
        h = step_now * per_chunk + inside
        both_x = dot(table, x_ref[inside])
        both_g = dot(table, g_ref[inside])
        coded_x, scale_x = code(both_x[:rows] + both_x[rows:])
        coded_g, scale_g = code(both_g[:rows] + both_g[rows:])
        scale_g = scale_g * factor_ref[...]
        for target in range(group):
            at = slice(target * own, (target + 1) * own)
            send[target, h] = jnp.concatenate([coded_x[at], coded_g[at]], axis=0).astype(jnp.int16)
            scales[target, 0:own] = jnp.where(lanes == h, scale_x[at], scales[target, 0:own])
            scales[target, own : 2 * own] = jnp.where(
                lanes == h, scale_g[at], scales[target, own : 2 * own]
            )
    for step in range(1, group):
        sums_copy(step_now, step, False).start()
    own_copy(step_now).start()

    @pl.when(step_now == chunks - 1)
    def _():
        for step in range(1, group):
            scales_copy(step, False).start()
        scale_own = pltpu.make_async_copy(scales.at[me], scales_ref.at[me], scale_own_sem)
        scale_own.start()

        def finish(chunk, carry):
            for step in range(1, group):
                sums_copy(chunk, step, False).wait_send()
                sums_copy(chunk, step, True).wait_recv()
            own_copy(chunk).wait()
            return carry

        lax.fori_loop(0, chunks, finish, 0)
        for step in range(1, group):
            scales_copy(step, False).wait_send()
            scales_copy(step, True).wait_recv()
        scale_own.wait()


def gelu_and_slope(values):
    root = math.sqrt(2.0 / math.pi)
    square = values * values
    tanh = jnp.tanh(root * (values + 0.044715 * (square * values)))
    half = 0.5 * (1.0 + tanh)
    slope = half + 0.5 * values * (1.0 - tanh * tanh) * (root * (1.0 + 3.0 * 0.044715 * square))
    return values * half, slope


def spectral_kernel(
    group, lat_count, sums_ref, scales_ref, there_high, there_low, back_high, back_low,
    first_ref, second_ref, bias_ref, mask_ref,
    coded_ref, coded_scales_ref, first_grad_ref, second_grad_ref, bias_grad_ref,
    line, send, scales, send_sem, recv_sem, own_sem, scale_send_sem, scale_recv_sem, scale_own_sem,
):
    me = place(lat_count)
    lon_count = group // lat_count
    lat_rows, mode_rows, chans = sums_ref.shape[1:]
    greet(group, lat_count)

    def gather(h, carry):
        for part in range(lat_count):
            total = None
            for lon in range(lon_count):
                source = lon * lat_count + part
                term = sums_ref[source, h].astype(jnp.int32).astype(jnp.float32) * pick(
                    scales_ref[source], h
                )
                total = term if total is None else total + term
            start = pl.multiple_of((part * lat_rows + h) * mode_rows, mode_rows)
            line[pl.ds(start, mode_rows), :] = total
        return carry

    lax.fori_loop(0, lat_rows, gather, 0)
    fields = dot_both((there_high[...], there_low[...]), split(line[...]))
    rows = fields.shape[0] // 4
    mask = mask_ref[...]
    spec = jnp.concatenate([fields[:rows], fields[rows : 2 * rows]], axis=1)
    out = jnp.concatenate(
        [fields[2 * rows : 3 * rows] * mask, fields[3 * rows :] * mask], axis=1
    )
    turned = ((1,), (1,))
    pre = dot_exact_right(spec, first_ref[...]) + bias_ref[...]
    act, slope = gelu_and_slope(pre)
    pre_grad = dot_exact_right(out, second_ref[...], turned) * slope
    spec_grad = dot_exact_right(pre_grad, first_ref[...], turned)
    spec_grad = jnp.concatenate([spec_grad[:, :chans], spec_grad[:, chans:]], axis=0)
    back = dot_both((back_high[...], back_low[...]), split(spec_grad))
    coded, scale = code(back)
    pairs = send.shape[1]
    send[...] = coded.astype(jnp.int16).reshape(send.shape)
    lanes = lax.broadcasted_iota(jnp.int32, (16, 128), 1)
    for part in range(lat_count):
        packed = jnp.zeros((16, 128), jnp.float32)
        for pair in range(pairs):
            start = (part * pairs + pair) * 16
            packed = jnp.where(lanes == pair, scale[start : start + 16], packed)
        scales[part] = packed

    def copies(step, arriving):
        target = lax.rem(me + step, group)
        part = lax.rem(target, lat_count)
        slot = lax.rem(me + group - step, group) if arriving else me
        return [
            pltpu.make_async_remote_copy(
                src_ref=source.at[part],
                dst_ref=landing.at[slot],
                send_sem=sent.at[step],
                recv_sem=arrived.at[step],
                device_id=device(target, lat_count),
                device_id_type=MESH,
            )
            for source, landing, sent, arrived in (
                (send, coded_ref, send_sem, recv_sem),
                (scales, coded_scales_ref, scale_send_sem, scale_recv_sem),
            )
        ]

    for step in range(1, group):
        for copy in copies(step, False):
            copy.start()
    my_part = lax.axis_index("lat")
    own = pltpu.make_async_copy(send.at[my_part], coded_ref.at[me], own_sem)
    own_scale = pltpu.make_async_copy(scales.at[my_part], coded_scales_ref.at[me], scale_own_sem)
    own.start()
    own_scale.start()

    def weight_grad(left, right):
        left = jnp.concatenate([left[:, :chans], left[:, chans:]], axis=0)
        right_real, right_imag = right[:, :chans], right[:, chans:]
        right = jnp.concatenate(
            [
                jnp.concatenate([right_real, right_imag], axis=1),
                jnp.concatenate([right_imag, -right_real], axis=1),
            ],
            axis=0,
        )
        return dot_both(split(left), split(right), ((0,), (0,)))

    first_grad_ref[...] = weight_grad(spec, pre_grad)
    second_grad_ref[...] = weight_grad(act, out)
    bias_grad_ref[0:1] = jnp.sum(pre_grad, axis=0, keepdims=True)
    bias_grad_ref[1:2] = jnp.sum(out, axis=0, keepdims=True)
    for step in range(1, group):
        for copy in copies(step, False):
            copy.wait_send()
        for copy in copies(step, True):
            copy.wait_recv()
    own.wait()
    own_scale.wait()


def inverse_kernel(table_ref, coded_ref, scales_ref, out_ref):
    scale = pick(scales_ref[...], pl.program_id(0))
    values = coded_ref[:, 0].astype(jnp.int32).astype(jnp.float32) * scale
    group, rows, chans = values.shape
    for inside in range(2):
        part = values[:, inside * rows // 2 : (inside + 1) * rows // 2].reshape(
            group * rows // 2, chans
        )
        high, low = split(part)
        out_ref[inside] = dot(
            table_ref[...], jnp.concatenate([high, low, high], axis=0)
        ).astype(jnp.bfloat16)


def block_diagonal(weights):
    blocks, _, size, _ = weights.shape

    def spread(part):
        eye = jnp.eye(blocks, dtype=part.dtype)
        full = part[:, :, None, :] * eye[:, None, :, None]
        return full.reshape(blocks * size, blocks * size)

    real, imag = spread(weights[:, 0]), spread(weights[:, 1])
    return jnp.concatenate(
        [jnp.concatenate([real, imag], axis=1), jnp.concatenate([-imag, real], axis=1)], axis=0
    )


def diagonal_blocks(grad, blocks, size):
    whole = grad.reshape(blocks, size, 2, blocks, size)
    return jnp.stack([jnp.swapaxes(whole[b, :, :, b], 0, 1) for b in range(blocks)])


def on_device_coded(
    inputs, cotangent, first_weight, first_bias, second_weight, counts, keep_flags
):
    lat_rows, lon_cells, chans = inputs.shape
    lon_count, lat_count = lax.axis_size("lon"), lax.axis_size("lat")
    lon_place, lat_place = lax.axis_index("lon"), lax.axis_index("lat")
    group = lon_count * lat_count
    modes_lon = KM // lon_count
    modes_own = KM // group
    lat_total = lat_rows * lat_count
    mine = first_weight.shape[1]
    size = first_weight.shape[-1]
    blocks = mine * lat_count
    vmem = pl.BlockSpec(memory_space=pltpu.VMEM)
    hbm = pl.BlockSpec(memory_space=pl.ANY)

    lon_high, lon_low = np_split(lon_table(lon_cells * lon_count))
    table = np.concatenate([lon_high, lon_low], axis=0)
    table = table.reshape(4 * KM, lon_count, lon_cells).transpose(1, 0, 2)
    table = lax.dynamic_index_in_dim(jnp.asarray(table), lon_place, 0, keepdims=False)
    table_back = np.concatenate([lon_high, lon_high, lon_low], axis=0).T
    table_back = table_back.reshape(lon_count, lon_cells, 6 * KM)
    table_back = lax.dynamic_index_in_dim(jnp.asarray(table_back), lon_place, 0, keepdims=False)
    there, back = lat_tables(lat_total, modes_own)
    factor = np.full((2 * KM, 1), 2.0, np.float32)
    factor[:2] = 1.0

    own_modes = lon_place * modes_lon + jnp.arange(modes_lon, dtype=jnp.int32)
    cut = own_modes[:, None] < counts[0][None, :]
    mask = jnp.where(cut[None], keep_flags[:, :, 0, :].astype(jnp.float32), 0.0)
    small = jnp.concatenate([mask.reshape(-1), first_bias.reshape(-1)])
    small = lax.all_gather(small, "lat", axis=0)
    weights = lax.all_gather(jnp.stack([first_weight[0], second_weight[0]]), "lat", axis=1, tiled=True)
    mask = small[:, : mask.size].reshape(lat_count, lat_total, modes_lon, mine)
    mask = lax.dynamic_slice_in_dim(mask, lat_place * modes_own, modes_own, 2)
    mask = jnp.transpose(mask, (2, 1, 0, 3)).reshape(modes_own * lat_total, blocks)
    mask = jnp.repeat(mask, size, axis=1)
    bias = small[:, -first_bias.size :].reshape(blocks, 2, size)
    bias = jnp.transpose(bias, (1, 0, 2)).reshape(1, 2 * chans)
    first, second = block_diagonal(weights[0]), block_diagonal(weights[1])

    per_chunk = 4
    chunks = lat_rows // per_chunk
    rows = 4 * modes_own
    dma = pltpu.SemaphoreType.DMA
    block = pl.BlockSpec((per_chunk, lon_cells, chans), lambda i: (i, 0, 0))
    sums, scales = pl.pallas_call(
        functools.partial(forward_kernel, group, lat_count, chunks),
        grid=(chunks,),
        out_shape=(
            jax.ShapeDtypeStruct((group, lat_rows, rows, chans), jnp.int16),
            jax.ShapeDtypeStruct((group, rows, 128), jnp.float32),
        ),
        in_specs=[
            pl.BlockSpec(table.shape, lambda i: (0, 0)),
            pl.BlockSpec(factor.shape, lambda i: (0, 0)),
            block,
            block,
        ],
        out_specs=(hbm, hbm),
        scratch_shapes=[
            pltpu.VMEM((group, lat_rows, rows, chans), jnp.int16),
            pltpu.VMEM((group, rows, 128), jnp.float32),
            dma((chunks, group)),
            dma((chunks, group)),
            dma((chunks,)),
            dma((group,)),
            dma((group,)),
            dma,
        ],
        compiler_params=pltpu.CompilerParams(
            collective_id=0, has_side_effects=True, vmem_limit_bytes=40 * 2**20
        ),
        cost_estimate=pl.CostEstimate(
            flops=16 * KM * inputs.size, bytes_accessed=4 * inputs.size, transcendentals=0
        ),
    )(table, jnp.asarray(factor), inputs, cotangent)

    pairs = lat_rows // 2
    coded, coded_scales, first_grad, second_grad, bias_grad = pl.pallas_call(
        functools.partial(spectral_kernel, group, lat_count),
        out_shape=(
            jax.ShapeDtypeStruct((group, pairs, 4 * modes_own, chans), jnp.int16),
            jax.ShapeDtypeStruct((group, 16, 128), jnp.float32),
            jax.ShapeDtypeStruct((chans, 2 * chans), jnp.float32),
            jax.ShapeDtypeStruct((chans, 2 * chans), jnp.float32),
            jax.ShapeDtypeStruct((2, 2 * chans), jnp.float32),
        ),
        in_specs=[vmem] * 10,
        out_specs=(hbm, hbm, vmem, vmem, vmem),
        scratch_shapes=[
            pltpu.VMEM((4 * modes_own * lat_total, chans), jnp.float32),
            pltpu.VMEM((lat_count, pairs, 4 * modes_own, chans), jnp.int16),
            pltpu.VMEM((lat_count, 16, 128), jnp.float32),
            dma((group,)),
            dma((group,)),
            dma,
            dma((group,)),
            dma((group,)),
            dma,
        ],
        compiler_params=pltpu.CompilerParams(
            collective_id=1, has_side_effects=True, vmem_limit_bytes=56 * 2**20
        ),
    )(
        sums,
        scales,
        *(jnp.asarray(part) for part in np_split(there)),
        *(jnp.asarray(part) for part in np_split(back)),
        first,
        second,
        bias,
        mask,
    )

    grads = jnp.stack(
        [diagonal_blocks(first_grad, blocks, size), diagonal_blocks(second_grad, blocks, size)]
    )
    bias_grads = jnp.transpose(bias_grad.reshape(2, 2, blocks, size), (0, 2, 1, 3))
    grads = jnp.concatenate([grads, bias_grads[:, :, :, None, :]], axis=3)
    grads = lax.psum(grads, ("lon", "lat"))
    grads = lax.dynamic_slice_in_dim(grads, lat_place * mine, mine, 1)

    input_grad = pl.pallas_call(
        inverse_kernel,
        grid=(pairs,),
        out_shape=jax.ShapeDtypeStruct(inputs.shape, jnp.bfloat16),
        in_specs=[
            pl.BlockSpec(table_back.shape, lambda i: (0, 0)),
            pl.BlockSpec((group, 1, 4 * modes_own, chans), lambda i: (0, i, 0, 0)),
            pl.BlockSpec((group, 16, 128), lambda i: (0, 0, 0)),
        ],
        out_specs=pl.BlockSpec((2, lon_cells, chans), lambda i: (i, 0, 0)),
        compiler_params=pltpu.CompilerParams(vmem_limit_bytes=32 * 2**20),
        cost_estimate=pl.CostEstimate(
            flops=12 * KM * inputs.size, bytes_accessed=2 * inputs.size, transcendentals=0
        ),
    )(table_back, coded, coded_scales)
    return (
        input_grad,
        grads[0][None, :, :, :size],
        grads[1][None, :, :, :size],
        grads[0][None, :, :, size],
        grads[1][None, :, :, size],
    )


def solution(mesh):
    group = mesh.shape["lon"] * mesh.shape["lat"]
    body = on_device_coded if KM == 4 * group else on_device
    return jax.shard_map(
        body,
        mesh=mesh,
        in_specs=(
            P(("ens", "lat"), "lon", "ch"),
            P(("ens", "lat"), "lon", "ch"),
            P("ch", "lat", None, None, None),
            P("ch", "lat", None, None),
            P("ch", "lat", None, None, None),
            P("ch", "lat"),
            P(None, "lon", "ch", "lat"),
        ),
        out_specs=(
            P(("ens", "lat"), "lon", "ch"),
            P(("ens", "ch"), "lat", None, None, None),
            P(("ens", "ch"), "lat", None, None, None),
            P(("ens", "ch"), "lat", None, None),
            P(("ens", "ch"), "lat", None, None),
        ),
        check_vma=False,
    )
```

profile of v0, /device:TPU:0, one launch (start us, length us, event | category | flops | bytes accessed | tf_op | source)
XLA Modules:
  0.0 258.7 jit_solution(3293585240704256185)
XLA Ops:
  7.2 0.0 all-reduce.2.cloned.1.call-start
  7.2 0.8 reshape.102
  8.0 0.7 convert_element_type.24
  8.7 0.7 broadcast_compare_fusion
  9.5 0.2 broadcast_in_dim.33
  9.6 0.2 copy.41
  9.8 0.2 convert_element_type.25
  10.0 5.2 %all-gather.1 = f32[2,1,1408]{2,1,0:T(1,128)S(1)} all-gather(f32[1,1,1408]{2,1,0:T(1,128)S(1)} %reshape.112), channel_id=2, replica_groups=mesh['ens'=2,'lon'=4,'lat'=2,'ch'=2] {'lat'}, dimensions={0}, use_global_device_ids=true | all-gather | bytes 16896 | tf_op jit(solution)/shard_map/all_gather | solution.py:534
  15.3 1.0 pad_maximum_fusion.1
  16.3 6.5 %all_gather.9 = bf16[2,4,2,96,96]{4,3,2,1,0:T(8,128)(2,1)S(1)} all-gather(bf16[2,2,2,96,96]{4,3,2,1,0:T(8,128)(2,1)S(1)} %pad_maximum_fusion.1), channel_id=1, replica_groups=mesh['ens'=2,'lon'=4,'lat'=2,'ch'=2] {'lat'}, dimensions={1}, use_global_device_ids=true | all-gather | bytes 442368 | tf_op jit(solution)/shard_map/all_gather | solution.py:535
  22.8 0.1 reshape.103
  22.9 0.7 reshape.104.bias_ref
  23.5 0.5 reshape.105
  24.0 0.1 dynamic-slice_bitcast_fusion.1
  24.1 0.1 copy.43
  24.2 0.1 reshape.106
  24.4 0.9 copy.44.mask_ref
  25.3 0.8 broadcast_multiply_fusion
  26.2 0.3 mul.101
  26.5 0.3 mul.93
  26.7 0.1 neg.6
  26.8 0.1 neg.7
  26.9 0.3 mul.97
  27.1 0.3 mul.89
  27.4 1.0 dynamic-slice_bitcast_fusion.2.table_ref
  28.4 0.0 copy-start.4
  28.4 1.1 maximum_maximum_fusion.1.second_ref
  29.5 1.1 maximum_maximum_fusion.first_ref
  30.6 0.0 copy-done.4
  30.6 77.9 %shard_map.176 = (s16[8,32,16,384]{3,2,1,0:T(8,128)(2,1)S(1)}, f32[8,16,128]{2,1,0:T(8,128)S(1)}) custom-call(bf16[128,1024]{1,0:T(8,128)(2,1)S(1)} %dynamic-slice_bitcast_fusion.2.table_ref, f32[64,1]{1,0:T(8,128)S(1)} %copy-done.4, bf16[32,1024,384]{2,1,0:T(8,128)(2,1)} %x_ref.1, bf16[32,1024,384]{2,1,0:T(8,128)(2,1)} %g_ref.1), custom_call_target="tpu_custom_call" | custom-call | flops 6442450944 | bytes 50331648 | tf_op jit(solution)/shard_map/pallas_call | solution.py:549
  108.5 0.0 copy-start
  108.5 1.7 copy-done
  110.2 0.0 copy-start.3
  110.2 0.6 copy-done.3
  110.8 44.6 %shard_map.177 = (s16[8,16,16,384]{3,2,1,0:T(8,128)(2,1)}, f32[8,16,128]{2,1,0:T(8,128)}, f32[384,768]{1,0:T(8,128)}, f32[384,768]{1,0:T(8,128)}, f32[2,768]{1,0:T(2,128)}) custom-call(s16[8,32,16,384]{3,2,1,0:T(8,128)(2,1)} %copy-done, f32[8,16,128]{2,1,0:T(8,128)} %copy-done.3, bf16[1024,1024]{1,0:T(8,128)(2,1)} %constant.44.clone.there_high, ...), custom_call_target="tpu_custom_call" | custom-call | tf_op jit(solution)/shard_map/pallas_call | solution.py:582
  155.4 0.8 reshape.110
  156.2 0.0 copy-start.5
  156.2 2.8 %reshape.108 = f32[4,96,2,4,96]{4,3,2,1,0:T(4,128)S(1)} reshape(f32[384,768]{1,0:T(8,128)} %get-tuple-element.16) | data formatting | bytes 2359296 | tf_op jit(solution)/shard_map/reshape | solution.py:499
  159.0 0.4 fusion.1
  159.5 0.0 copy-done.5
  159.5 1.6 reshape.109
  161.1 0.4 fusion.2
  161.6 0.0 copy-start.1
  161.6 0.0 copy-start.2
  161.7 1.0 pad_maximum_fusion
  162.6 0.0 all-reduce.2.cloned.1.call-update
  162.7 1.1 dynamic-slice_bitcast_fusion.table_ref
  163.8 0.0 copy-done.1
  163.8 0.0 copy-done.2
  163.8 16.3 %shard_map.178 = bf16[32,1024,384]{2,1,0:T(8,128)(2,1)} custom-call(bf16[1024,192]{1,0:T(8,128)(2,1)S(1)} %dynamic-slice_bitcast_fusion.table_ref, s16[8,16,16,384]{3,2,1,0:T(8,128)(2,1)S(1)} %copy-done.1, f32[8,16,128]{2,1,0:T(8,128)S(1)} %copy-done.2), custom_call_target="tpu_custom_call" | custom-call | flops 4831838208 | bytes 25165824 | tf_op jit(solution)/shard_map/pallas_call | solution.py:626
  180.1 68.2 %all-reduce.2.cloned.1.call-done = f32[2,4,2,97,96]{4,3,2,1,0:T(8,128)} async-done(((f32[2,4,2,97,96]{4,3,2,1,0:T(8,128)}), f32[2,4,2,97,96]{4,3,2,1,0:T(8,128)}) %all-reduce.2.cloned.1.call-update) | async-done | bytes 595984 | tf_op jit(solution)/shard_map/psum | solution.py:623
  248.3 1.1 dynamic-slice_bitcast_fusion.3
  249.3 0.6 slice.109
  249.9 0.7 slice_bitcast_fusion
  250.6 0.6 slice.108
  251.2 0.7 slice_bitcast_fusion.1
  (24 shorter events, 0.3 us)
Async XLA Ops:
  7.2 241.1 %all-reduce.2.cloned.1.call-start = ((), (), s32[]{:S(2)}) async-start(), calls=%async_computation | async-start | bytes 1703936 | tf_op jit(solution)/shard_map/psum | solution.py:623
  28.4 2.2 copy-start.4
  108.5 1.7 copy-start
  110.2 0.6 copy-start.3
  156.2 3.2 %copy-start.5 = (f32[384,768]{1,0:T(8,128)S(1)}, f32[384,768]{1,0:T(8,128)}, u32[]{:S(2)}) copy-start(f32[384,768]{1,0:T(8,128)} %get-tuple-element.17) | copy-start | bytes 3538948
  161.6 2.2 copy-start.1
  161.6 2.2 copy-start.2
Sparse Core Ops, SparseCore 0:
  162.8 85.4 all-reduce.1
where the time goes:
time: 259 us
  Pallas kernels  139 us (54%)
  waiting for transfers between devices  68.2 us (26%)
  local copies, waits for them, and re-layouts  18.9 us (7%)
  between operations  14.4 us (6%)
  blocking collectives  11.7 us (5%)
  other arithmetic  6.66 us (3%)
    pallas_call x1, Pallas kernels, on_device_coded(): pl.pallas_call(functools.partial(forward_kernel, group, lat_count, chunks...  77.9 us
    psum x1, waiting for transfers between devices, on_device_coded(): grads = lax.psum(grads, ('lon', 'lat'))  68.2 us
    pallas_call x1, Pallas kernels, on_device_coded(): pl.pallas_call(functools.partial(spectral_kernel, group, lat_count), out_...  44.6 us
    pallas_call x1, Pallas kernels, on_device_coded(): pl.pallas_call(inverse_kernel, grid=(pairs,), out_shape=jax.ShapeDtypeStr...  16.3 us
    all_gather x1, blocking collectives, on_device_coded(): lax.all_gather(jnp.stack([first_weight[0], second_weight[0]]), 'lat', axi...  6.46 us
    all_gather x1, blocking collectives, on_device_coded(): small = lax.all_gather(small, 'lat', axis=0)  5.25 us
  transfers between devices with their start and end apart: 1, of which 1 were waited for; matrix products, arithmetic and copies ran while one was open for 0% of the time, Pallas kernels for 6%

commit v1 on v0

--- a/solution.py
+++ b/solution.py
@@ -271,8 +271,10 @@
 
 
 def forward_kernel(
-    group, lat_count, chunks, table_ref, factor_ref, x_ref, g_ref, sums_ref, scales_ref,
+    group, lat_count, chunks, table_ref, factor_ref, weights_ref, small_ref, x_ref, g_ref,
+    sums_ref, scales_ref, all_weights_ref, all_small_ref,
     send, scales, send_sem, recv_sem, own_sem, scale_send_sem, scale_recv_sem, scale_own_sem,
+    side_send_sem, side_recv_sem, side_own_sem,
 ):
     step_now = pl.program_id(0)
     me = place(lat_count)
@@ -309,9 +311,38 @@
             device_id_type=MESH,
         )
 
+    sides = ((weights_ref, all_weights_ref), (small_ref, all_small_ref))
+    my_part = lax.axis_index("lat")
+
+    def side_copies(step, arriving):
+        target = lax.rem(my_part + step, lat_count)
+        slot = lax.rem(my_part + lat_count - step, lat_count) if arriving else my_part
+        return [
+            pltpu.make_async_remote_copy(
+                src_ref=source,
+                dst_ref=landing.at[slot],
+                send_sem=side_send_sem.at[which, step],
+                recv_sem=side_recv_sem.at[which, step],
+                device_id={"lat": target},
+                device_id_type=MESH,
+            )
+            for which, (source, landing) in enumerate(sides)
+        ]
+
+    def side_own():
+        return [
+            pltpu.make_async_copy(source, landing.at[my_part], side_own_sem.at[which])
+            for which, (source, landing) in enumerate(sides)
+        ]
+
     @pl.when(step_now == 0)
     def _():
         greet(group, lat_count)
+        for step in range(1, lat_count):
+            for copy in side_copies(step, False):
+                copy.start()
+        for copy in side_own():
+            copy.start()
         scales[...] = jnp.zeros_like(scales)
 
     table = table_ref[...]
@@ -353,6 +384,26 @@
             scales_copy(step, False).wait_send()
             scales_copy(step, True).wait_recv()
         scale_own.wait()
+        for step in range(1, lat_count):
+            for copy in side_copies(step, False):
+                copy.wait_send()
+            for copy in side_copies(step, True):
+                copy.wait_recv()
+        for copy in side_own():
+            copy.wait()
+
+
+def code_rows(values):
+    most = jnp.maximum(jnp.max(jnp.abs(values), axis=1, keepdims=True), LEAST)
+    power = jnp.ceil(jnp.log(most) * (1.0 / math.log(2.0)) + 0.01)
+    lanes = lax.broadcasted_iota(jnp.int32, values.shape, 1)
+    coded = jnp.where(lanes == 127, power, jnp.round(values * jnp.exp2(15.0 - power)))
+    return coded.astype(jnp.int32).astype(jnp.int16)
+
+
+def decode_rows(coded):
+    values = coded.astype(jnp.int32).astype(jnp.float32)
+    return values * jnp.exp2(pick(values, 127) - 15.0)
 
 
 def gelu_and_slope(values):
@@ -367,8 +418,10 @@
 def spectral_kernel(
     group, lat_count, sums_ref, scales_ref, there_high, there_low, back_high, back_low,
     first_ref, second_ref, bias_ref, mask_ref,
-    coded_ref, coded_scales_ref, first_grad_ref, second_grad_ref, bias_grad_ref,
-    line, send, scales, send_sem, recv_sem, own_sem, scale_send_sem, scale_recv_sem, scale_own_sem,
+    coded_ref, coded_scales_ref, grads_ref,
+    line, send, scales, whole, piece, pieces, pieces_in, sums, send_sem, recv_sem, own_sem,
+    scale_send_sem, scale_recv_sem, scale_own_sem, piece_send_sem, piece_recv_sem,
+    sum_send_sem, sum_recv_sem,
 ):
     me = place(lat_count)
     lon_count = group // lat_count
@@ -454,10 +507,68 @@
         )
         return dot_both(split(left), split(right), ((0,), (0,)))
 
-    first_grad_ref[...] = weight_grad(spec, pre_grad)
-    second_grad_ref[...] = weight_grad(act, out)
-    bias_grad_ref[0:1] = jnp.sum(pre_grad, axis=0, keepdims=True)
-    bias_grad_ref[1:2] = jnp.sum(out, axis=0, keepdims=True)
+    size = (grads_ref.shape[1] - 16) // 2
+    mine = chans // size // lat_count
+    whole[0, :chans] = weight_grad(spec, pre_grad)
+    whole[1, :chans] = weight_grad(act, out)
+    for which, rows_in in enumerate((pre_grad, out)):
+        total = jnp.sum(rows_in, axis=0, keepdims=True)
+        first_row = lax.broadcasted_iota(jnp.int32, (8, 2 * chans), 0) == 0
+        whole[which, chans : chans + 8] = jnp.where(first_row, total, 0.0)
+    piece[...] = jnp.zeros_like(piece)
+    for target in range(group):
+        which, offset = divmod(target // lat_count, mine)
+        at = (target % lat_count * mine + offset) * size
+        for part in range(2):
+            lanes_at = slice(part * chans + at, part * chans + at + size)
+            piece[part * size : (part + 1) * size, 0:size] = whole[
+                which, at : at + size, lanes_at
+            ]
+            start = 2 * size + 8 * part
+            piece[start : start + 8, 0:size] = whole[which, chans : chans + 8, lanes_at]
+        pieces[target] = code_rows(piece[...])
+
+    def piece_copy(step):
+        target = lax.rem(me + step, group)
+        return pltpu.make_async_remote_copy(
+            src_ref=pieces.at[target],
+            dst_ref=pieces_in.at[step],
+            send_sem=piece_send_sem.at[step],
+            recv_sem=piece_recv_sem.at[step],
+            device_id=device(target, lat_count),
+            device_id_type=MESH,
+        )
+
+    my_lon = lax.axis_index("lon")
+
+    def sum_copy(step, arriving):
+        slot = lax.rem(my_lon + lon_count - step, lon_count) if arriving else my_lon
+        return pltpu.make_async_remote_copy(
+            src_ref=sums.at[my_lon],
+            dst_ref=sums.at[slot],
+            send_sem=sum_send_sem.at[step],
+            recv_sem=sum_recv_sem.at[step],
+            device_id={"lon": lax.rem(my_lon + step, lon_count)},
+            device_id_type=MESH,
+        )
+
+    for step in range(1, group):
+        piece_copy(step).start()
+    total = decode_rows(pieces[me])
+    for step in range(1, group):
+        piece_copy(step).wait_recv()
+        total = total + decode_rows(pieces_in[step])
+    lanes = lax.broadcasted_iota(jnp.int32, total.shape, 1)
+    sums[my_lon] = code_rows(jnp.where(lanes < size, total, 0.0))
+    for step in range(1, lon_count):
+        sum_copy(step, False).start()
+    for step in range(1, group):
+        piece_copy(step).wait_send()
+    for step in range(1, lon_count):
+        sum_copy(step, False).wait_send()
+        sum_copy(step, True).wait_recv()
+    for lon in range(lon_count):
+        grads_ref[lon] = decode_rows(sums[lon])
     for step in range(1, group):
         for copy in copies(step, False):
             copy.wait_send()
@@ -493,11 +604,6 @@
     return jnp.concatenate(
         [jnp.concatenate([real, imag], axis=1), jnp.concatenate([-imag, real], axis=1)], axis=0
     )
-
-
-def diagonal_blocks(grad, blocks, size):
-    whole = grad.reshape(blocks, size, 2, blocks, size)
-    return jnp.stack([jnp.swapaxes(whole[b, :, :, b], 0, 1) for b in range(blocks)])
 
 
 def on_device_coded(
@@ -531,35 +637,32 @@
     cut = own_modes[:, None] < counts[0][None, :]
     mask = jnp.where(cut[None], keep_flags[:, :, 0, :].astype(jnp.float32), 0.0)
     small = jnp.concatenate([mask.reshape(-1), first_bias.reshape(-1)])
-    small = lax.all_gather(small, "lat", axis=0)
-    weights = lax.all_gather(jnp.stack([first_weight[0], second_weight[0]]), "lat", axis=1, tiled=True)
-    mask = small[:, : mask.size].reshape(lat_count, lat_total, modes_lon, mine)
-    mask = lax.dynamic_slice_in_dim(mask, lat_place * modes_own, modes_own, 2)
-    mask = jnp.transpose(mask, (2, 1, 0, 3)).reshape(modes_own * lat_total, blocks)
-    mask = jnp.repeat(mask, size, axis=1)
-    bias = small[:, -first_bias.size :].reshape(blocks, 2, size)
-    bias = jnp.transpose(bias, (1, 0, 2)).reshape(1, 2 * chans)
-    first, second = block_diagonal(weights[0]), block_diagonal(weights[1])
-
+    used = small.size
+    small = jnp.pad(small, (0, -used % 1024)).reshape(-1, 128)
+    weights = jnp.stack([first_weight[0], second_weight[0]])
     per_chunk = 4
     chunks = lat_rows // per_chunk
     rows = 4 * modes_own
     dma = pltpu.SemaphoreType.DMA
     block = pl.BlockSpec((per_chunk, lon_cells, chans), lambda i: (i, 0, 0))
-    sums, scales = pl.pallas_call(
+    sums, scales, weights, small = pl.pallas_call(
         functools.partial(forward_kernel, group, lat_count, chunks),
         grid=(chunks,),
         out_shape=(
             jax.ShapeDtypeStruct((group, lat_rows, rows, chans), jnp.int16),
             jax.ShapeDtypeStruct((group, rows, 128), jnp.float32),
+            jax.ShapeDtypeStruct((lat_count, *weights.shape), weights.dtype),
+            jax.ShapeDtypeStruct((lat_count, *small.shape), small.dtype),
         ),
         in_specs=[
             pl.BlockSpec(table.shape, lambda i: (0, 0)),
             pl.BlockSpec(factor.shape, lambda i: (0, 0)),
+            hbm,
+            hbm,
             block,
             block,
         ],
-        out_specs=(hbm, hbm),
+        out_specs=(hbm,) * 4,
         scratch_shapes=[
             pltpu.VMEM((group, lat_rows, rows, chans), jnp.int16),
             pltpu.VMEM((group, rows, 128), jnp.float32),
@@ -569,6 +672,9 @@
             dma((group,)),
             dma((group,)),
             dma,
+            dma((2, lat_count)),
+            dma((2, lat_count)),
+            dma((2,)),
         ],
         compiler_params=pltpu.CompilerParams(
             collective_id=0, has_side_effects=True, vmem_limit_bytes=40 * 2**20
@@ -576,30 +682,48 @@
         cost_estimate=pl.CostEstimate(
             flops=16 * KM * inputs.size, bytes_accessed=4 * inputs.size, transcendentals=0
         ),
-    )(table, jnp.asarray(factor), inputs, cotangent)
+    )(table, jnp.asarray(factor), weights, small, inputs, cotangent)
+
+    small = small.reshape(lat_count, -1)[:, :used]
+    mask = small[:, : mask.size].reshape(lat_count, lat_total, modes_lon, mine)
+    mask = lax.dynamic_slice_in_dim(mask, lat_place * modes_own, modes_own, 2)
+    mask = jnp.transpose(mask, (2, 1, 0, 3)).reshape(modes_own * lat_total, blocks)
+    mask = jnp.repeat(mask, size, axis=1)
+    bias = small[:, -first_bias.size :].reshape(blocks, 2, size)
+    bias = jnp.transpose(bias, (1, 0, 2)).reshape(1, 2 * chans)
+    first = block_diagonal(weights[:, 0].reshape(blocks, 2, size, size))
+    second = block_diagonal(weights[:, 1].reshape(blocks, 2, size, size))
 
     pairs = lat_rows // 2
-    coded, coded_scales, first_grad, second_grad, bias_grad = pl.pallas_call(
+    piece = (2 * size + 16, 128)
+    coded, coded_scales, grads = pl.pallas_call(
         functools.partial(spectral_kernel, group, lat_count),
         out_shape=(
             jax.ShapeDtypeStruct((group, pairs, 4 * modes_own, chans), jnp.int16),
             jax.ShapeDtypeStruct((group, 16, 128), jnp.float32),
-            jax.ShapeDtypeStruct((chans, 2 * chans), jnp.float32),
-            jax.ShapeDtypeStruct((chans, 2 * chans), jnp.float32),
-            jax.ShapeDtypeStruct((2, 2 * chans), jnp.float32),
+            jax.ShapeDtypeStruct((lon_count, *piece), jnp.float32),
         ),
         in_specs=[vmem] * 10,
-        out_specs=(hbm, hbm, vmem, vmem, vmem),
+        out_specs=(hbm, hbm, vmem),
         scratch_shapes=[
             pltpu.VMEM((4 * modes_own * lat_total, chans), jnp.float32),
             pltpu.VMEM((lat_count, pairs, 4 * modes_own, chans), jnp.int16),
             pltpu.VMEM((lat_count, 16, 128), jnp.float32),
+            pltpu.VMEM((2, chans + 8, 2 * chans), jnp.float32),
+            pltpu.VMEM(piece, jnp.float32),
+            pltpu.VMEM((group, *piece), jnp.int16),
+            pltpu.VMEM((group, *piece), jnp.int16),
+            pltpu.VMEM((lon_count, *piece), jnp.int16),
             dma((group,)),
             dma((group,)),
             dma,
             dma((group,)),
             dma((group,)),
             dma,
+            dma((group,)),
+            dma((group,)),
+            dma((lon_count,)),
+            dma((lon_count,)),
         ],
         compiler_params=pltpu.CompilerParams(
             collective_id=1, has_side_effects=True, vmem_limit_bytes=56 * 2**20
@@ -615,13 +739,8 @@
         mask,
     )
 
-    grads = jnp.stack(
-        [diagonal_blocks(first_grad, blocks, size), diagonal_blocks(second_grad, blocks, size)]
-    )
-    bias_grads = jnp.transpose(bias_grad.reshape(2, 2, blocks, size), (0, 2, 1, 3))
-    grads = jnp.concatenate([grads, bias_grads[:, :, :, None, :]], axis=3)
-    grads = lax.psum(grads, ("lon", "lat"))
-    grads = lax.dynamic_slice_in_dim(grads, lat_place * mine, mine, 1)
+    weight_grads = grads[:, : 2 * size, :size].reshape(2, 1, mine, 2, size, size)
+    bias_grads = grads[:, 2 * size :: 8, :size].reshape(2, 1, mine, 2, size)
 
     input_grad = pl.pallas_call(
         inverse_kernel,
@@ -640,10 +759,10 @@
     )(table_back, coded, coded_scales)
     return (
         input_grad,
-        grads[0][None, :, :, :size],
-        grads[1][None, :, :, :size],
-        grads[0][None, :, :, size],
-        grads[1][None, :, :, size],
+        weight_grads[0],
+        weight_grads[1],
+        bias_grads[0],
+        bias_grads[1],
     )
 
 

time: 259 us -> 189 us (0.73)
  waiting for transfers between devices: 68.2 us -> 0 us
  Pallas kernels: 139 us -> 168 us
  between operations: 14.4 us -> 0.84 us
  blocking collectives: 11.7 us -> 0 us
  local copies, waits for them, and re-layouts: 18.9 us -> 14.6 us
    psum x1 -> x0, waiting for transfers between devices: 68.2 us -> none  [on_device_coded(): grads = lax.psum(grads, ('lon', 'lat'))]
    pallas_call x1, Pallas kernels: 44.6 us -> 70.1 us  [on_device_coded(): pl.pallas_call(functools.partial(spectral_kernel, group, lat_count), out_...]
    all_gather x2 -> x0, blocking collectives: 11.7 us -> none  [the longest x1 6.46 us: on_device_coded(): lax.all_gather(jnp.stack([first_weight[0], second_weight[0]]), 'lat', axi...]
    reshape x4 -> x0, local copies, waits for them, and re-layouts: 5.14 us -> none  [the longest x2 4.35 us: diagonal_blocks(): whole = grad.reshape(blocks, size, 2, blocks, size)]
    pallas_call x1, Pallas kernels: 77.9 us -> 81.4 us  [on_device_coded(): pl.pallas_call(functools.partial(forward_kernel, group, lat_count, chunks...]
  transfers between devices with their start and end apart: 1 -> 0, of which waited for: 1 -> 0; matrix products, arithmetic and copies ran while one was open for 0% -> 0% of each run, Pallas kernels for 6% -> 0%
where the time goes in v1:
time: 189 us
  Pallas kernels  168 us (89%)
  local copies, waits for them, and re-layouts  14.6 us (8%)
  other arithmetic  5.63 us (3%)
    pallas_call x1, Pallas kernels, on_device_coded(): pl.pallas_call(functools.partial(forward_kernel, group, lat_count, chunks...  81.4 us
    pallas_call x1, Pallas kernels, on_device_coded(): pl.pallas_call(functools.partial(spectral_kernel, group, lat_count), out_...  70.1 us
    pallas_call x1, Pallas kernels, on_device_coded(): pl.pallas_call(inverse_kernel, grid=(pairs,), out_shape=jax.ShapeDtypeStr...  16.3 us
    unnamed x11, local copies, waits for them, and re-layouts  4.55 us

profile of v1, /device:TPU:0, one launch (start us, length us, event | category | flops | bytes accessed | tf_op | source)
XLA Modules:
  0.0 188.9 jit_solution(14407913674440929337)
XLA Ops:
  0.6 0.0 copy-start.4
  0.7 0.7 broadcast_compare_fusion
  1.4 0.8 reshape.109
  2.2 0.7 convert_element_type.25
  2.9 0.2 broadcast_in_dim.24
  3.1 1.0 pad_maximum_fusion.weights_ref
  4.1 0.2 copy.20
  4.2 0.2 convert_element_type.26
  4.4 1.0 dynamic-slice_bitcast_fusion.2.table_ref
  5.4 1.1 dynamic-slice_bitcast_fusion.table_ref
  6.5 0.0 copy-done.4
  6.5 81.4 %shard_map.176 = (s16[8,32,16,384]{3,2,1,0:T(8,128)(2,1)S(1)}, f32[8,16,128]{2,1,0:T(8,128)S(1)}, bf16[2,2,2,2,96,96]{5,4,3,2,1,0:T(8,128)(2,1)S(1)}, f32[2,16,128]{2,1,0:T(8,128)S(1)}) custom-call(bf16[128,1024]{1,0:T(8,128)(2,1)S(1)} %dynamic-slice_bitcast_fusion.2.table_ref, f32[64,1]{1,0:T(8,128)S(1)} %copy-done.4, ...), custom_call_target="tpu_custom_call" | custom-call | flops 6442450944 | bytes 50331648 | tf_op jit(solution)/shard_map/pallas_call | solution.py:648
  87.9 0.0 copy-start
  87.9 1.7 copy-done
  89.5 0.0 copy-start.2
  89.5 0.6 copy-done.2
  90.2 0.1 reshape.112
  90.3 0.7 reshape.113.bias_ref
  91.0 0.5 reshape.114
  91.5 0.1 dynamic-slice_bitcast_fusion.1
  91.6 0.1 copy.22
  91.7 0.1 reshape.115
  91.9 0.9 copy.23.mask_ref
  92.8 0.8 broadcast_multiply_fusion
  93.6 0.3 mul.99
  93.9 0.3 mul.91
  94.2 0.1 neg.6
  94.2 0.1 neg.7
  94.3 0.3 mul.95
  94.6 1.1 maximum_maximum_fusion.1.second_ref
  95.7 0.3 mul.87
  95.9 1.1 maximum_maximum_fusion.first_ref
  97.1 70.1 %shard_map.177 = (s16[8,16,16,384]{3,2,1,0:T(8,128)(2,1)}, f32[8,16,128]{2,1,0:T(8,128)}, f32[4,208,128]{2,1,0:T(8,128)}) custom-call(s16[8,32,16,384]{3,2,1,0:T(8,128)(2,1)} %copy-done, f32[8,16,128]{2,1,0:T(8,128)} %copy-done.2, bf16[1024,1024]{1,0:T(8,128)(2,1)} %constant.43.clone.there_high, bf16[1024,1024]{1,0:T(8,128)(2,1)} %constant.44.clone.there_low, ...), custom_call_target="tpu_custom_call" | custom-call | tf_op jit(solution)/shard_map/pallas_call | solution.py:699
  167.2 0.8 slice.59
  168.0 1.8 fusion.2
  169.8 0.6 slice_bitcast_fusion.4
  170.4 0.0 copy-start.1
  170.4 1.4 copy-done.1
  171.8 0.0 copy-start.3
  171.8 0.8 copy-done.3
  172.6 16.3 %shard_map.178 = bf16[32,1024,384]{2,1,0:T(8,128)(2,1)} custom-call(bf16[1024,192]{1,0:T(8,128)(2,1)S(1)} %dynamic-slice_bitcast_fusion.table_ref, s16[8,16,16,384]{3,2,1,0:T(8,128)(2,1)S(1)} %copy-done.1, f32[8,16,128]{2,1,0:T(8,128)S(1)} %copy-done.3), custom_call_target="tpu_custom_call" | custom-call | flops 4831838208 | bytes 25165824 | tf_op jit(solution)/shard_map/pallas_call | solution.py:745
  (12 shorter events, 0.2 us)
Async XLA Ops:
  0.6 5.9 %copy-start.4 = (f32[64,1]{1,0:T(8,128)S(1)}, f32[64,1]{1,0:T(8,128)}, u32[]{:S(2)}) copy-start(f32[64,1]{1,0:T(8,128)} %constant.42.clone.factor_ref) | copy-start | bytes 772
  87.9 1.7 copy-start
  89.5 0.6 copy-start.2
  170.4 1.4 copy-start.1
  171.8 0.8 copy-start.3

commit v2 on v1

--- a/solution.py
+++ b/solution.py
@@ -485,15 +485,6 @@
                 (scales, coded_scales_ref, scale_send_sem, scale_recv_sem),
             )
         ]
-
-    for step in range(1, group):
-        for copy in copies(step, False):
-            copy.start()
-    my_part = lax.axis_index("lat")
-    own = pltpu.make_async_copy(send.at[my_part], coded_ref.at[me], own_sem)
-    own_scale = pltpu.make_async_copy(scales.at[my_part], coded_scales_ref.at[me], scale_own_sem)
-    own.start()
-    own_scale.start()
 
     def weight_grad(left, right):
         left = jnp.concatenate([left[:, :chans], left[:, chans:]], axis=0)
@@ -554,6 +545,14 @@
 
     for step in range(1, group):
         piece_copy(step).start()
+    for step in range(1, group):
+        for copy in copies(step, False):
+            copy.start()
+    my_part = lax.axis_index("lat")
+    own = pltpu.make_async_copy(send.at[my_part], coded_ref.at[me], own_sem)
+    own_scale = pltpu.make_async_copy(scales.at[my_part], coded_scales_ref.at[me], scale_own_sem)
+    own.start()
+    own_scale.start()
     total = decode_rows(pieces[me])
     for step in range(1, group):
         piece_copy(step).wait_recv()

time: 189 us -> 191 us (1.011)
  no operation moved by 1% of the time
where the time goes in v2:
time: 191 us; the launch traced here: 190 us
  Pallas kernels  169 us (88%)
  local copies, waits for them, and re-layouts  14.6 us (8%)
  other arithmetic  5.63 us (3%)
    pallas_call x1, Pallas kernels, on_device_coded(): pl.pallas_call(functools.partial(forward_kernel, group, lat_count, chunks...  81.4 us
    pallas_call x1, Pallas kernels, on_device_coded(): pl.pallas_call(functools.partial(spectral_kernel, group, lat_count), out_...  71.4 us
    pallas_call x1, Pallas kernels, on_device_coded(): pl.pallas_call(inverse_kernel, grid=(pairs,), out_shape=jax.ShapeDtypeStr...  16.3 us
    unnamed x11, local copies, waits for them, and re-layouts  4.55 us

profile of v2, /device:TPU:0, one launch (start us, length us, event | category | flops | bytes accessed | tf_op | source)
XLA Modules:
  0.0 190.2 jit_solution(8648424095687690742)
XLA Ops:
  0.6 0.0 copy-start.4
  0.7 0.7 broadcast_compare_fusion
  1.4 0.8 reshape.109
  2.2 0.7 convert_element_type.25
  2.9 0.2 broadcast_in_dim.24
  3.1 1.0 pad_maximum_fusion.weights_ref
  4.1 0.2 copy.20
  4.2 0.2 convert_element_type.26
  4.4 1.0 dynamic-slice_bitcast_fusion.2.table_ref
  5.4 1.1 dynamic-slice_bitcast_fusion.table_ref
  6.5 0.0 copy-done.4
  6.5 81.4 %shard_map.176 = (s16[8,32,16,384]{3,2,1,0:T(8,128)(2,1)S(1)}, f32[8,16,128]{2,1,0:T(8,128)S(1)}, bf16[2,2,2,2,96,96]{5,4,3,2,1,0:T(8,128)(2,1)S(1)}, f32[2,16,128]{2,1,0:T(8,128)S(1)}) custom-call(bf16[128,1024]{1,0:T(8,128)(2,1)S(1)} %dynamic-slice_bitcast_fusion.2.table_ref, f32[64,1]{1,0:T(8,128)S(1)} %copy-done.4, ...), custom_call_target="tpu_custom_call" | custom-call | flops 6442450944 | bytes 50331648 | tf_op jit(solution)/shard_map/pallas_call | solution.py:647
  87.9 0.0 copy-start
  87.9 1.7 copy-done
  89.5 0.0 copy-start.2
  89.5 0.6 copy-done.2
  90.2 0.1 reshape.112
  90.3 0.7 reshape.113.bias_ref
  91.0 0.5 reshape.114
  91.5 0.1 dynamic-slice_bitcast_fusion.1
  91.6 0.1 copy.22
  91.7 0.1 reshape.115
  91.9 0.9 copy.23.mask_ref
  92.8 0.8 broadcast_multiply_fusion
  93.6 0.3 mul.99
  93.9 0.3 mul.91
  94.2 0.1 neg.6
  94.2 0.1 neg.7
  94.3 0.3 mul.95
  94.6 1.1 maximum_maximum_fusion.1.second_ref
  95.7 0.3 mul.87
  95.9 1.1 maximum_maximum_fusion.first_ref
  97.1 71.4 %shard_map.177 = (s16[8,16,16,384]{3,2,1,0:T(8,128)(2,1)}, f32[8,16,128]{2,1,0:T(8,128)}, f32[4,208,128]{2,1,0:T(8,128)}) custom-call(s16[8,32,16,384]{3,2,1,0:T(8,128)(2,1)} %copy-done, f32[8,16,128]{2,1,0:T(8,128)} %copy-done.2, bf16[1024,1024]{1,0:T(8,128)(2,1)} %constant.43.clone.there_high, bf16[1024,1024]{1,0:T(8,128)(2,1)} %constant.44.clone.there_low, ...), custom_call_target="tpu_custom_call" | custom-call | tf_op jit(solution)/shard_map/pallas_call | solution.py:698
  168.5 0.8 slice.59
  169.3 1.8 fusion.2
  171.0 0.6 slice_bitcast_fusion.4
  171.6 0.0 copy-start.1
  171.6 1.4 copy-done.1
  173.0 0.0 copy-start.3
  173.0 0.8 copy-done.3
  173.9 16.3 %shard_map.178 = bf16[32,1024,384]{2,1,0:T(8,128)(2,1)} custom-call(bf16[1024,192]{1,0:T(8,128)(2,1)S(1)} %dynamic-slice_bitcast_fusion.table_ref, s16[8,16,16,384]{3,2,1,0:T(8,128)(2,1)S(1)} %copy-done.1, f32[8,16,128]{2,1,0:T(8,128)S(1)} %copy-done.3), custom_call_target="tpu_custom_call" | custom-call | flops 4831838208 | bytes 25165824 | tf_op jit(solution)/shard_map/pallas_call | solution.py:744
  (12 shorter events, 0.2 us)
Async XLA Ops:
  0.6 5.9 %copy-start.4 = (f32[64,1]{1,0:T(8,128)S(1)}, f32[64,1]{1,0:T(8,128)}, u32[]{:S(2)}) copy-start(f32[64,1]{1,0:T(8,128)} %constant.42.clone.factor_ref) | copy-start | bytes 772
  87.9 1.7 copy-start
  89.5 0.6 copy-start.2
  171.6 1.4 copy-start.1
  173.0 0.8 copy-start.3
